TPU v7x, 256 devices: a whole 4x4x8 slice. The times are simulated.
256 devices in a mesh: emit: 32 (over y, z), panel: 8 (over x, core).
Axes of the slice: x: 4, y: 4, z: 8, core: 2. Of those that a mesh axis runs over, the one named last changes fastest.
Arguments:
- green_matrix: float32 [2, 196608, 1024], P(None, 'emit', 'panel'), may hold values from -120 to 120
- sign_bits: int32 [196608], P('emit'), may hold values from 0 to 1
- column_picks: int32 [1536], replicated, may hold values from 0 to 196607
Outputs:
- sketch: float32 [1536, 2, 1024], P('emit', None, 'panel')
All inputs are finite; a program needn't handle non-finite values.
Results may differ from a plain program's by a relative error of at most 0.000094.
Values sent between devices are 32-bit elements; how exact they have to be, the bound alone decides.
A program may use at most 128 MiB of HBM per device.

v0:
```python
import math

import jax
import jax.numpy as jnp
from jax import lax
from jax.sharding import PartitionSpec as P

N1 = 384
N2 = 512
EMITTERS = 196608


def phases(numerator, period):
    radians = -2.0 * math.pi / period * numerator.astype(jnp.float32)
    return (jnp.cos(radians), jnp.sin(radians))


def body(green_matrix, sign_bits, column_picks):
    rows_here = green_matrix.shape[2]
    groups = lax.axis_size("emit")
    block_b = N2 // groups
    block_a = N1 // groups
    position = lax.axis_index("emit")
    highest = lax.Precision.HIGHEST
    signed = green_matrix * (2 * sign_bits - 1).astype(jnp.float32)[None, :, None]
    freq_high = column_picks // N2
    freq_part = column_picks % N2
    blocked = signed.reshape(2, block_b, N1, rows_here)
    steps_b = jnp.arange(N2, dtype=jnp.int32)
    cos_b, sin_b = phases(steps_b[:, None] * steps_b[None, :] % N2, N2)
    local_a = position * block_a + jnp.arange(block_a, dtype=jnp.int32)
    twid_cos, twid_sin = phases(steps_b[:, None] * local_a[None, :] % EMITTERS, EMITTERS)
    portion = lax.all_to_all(blocked, "emit", split_axis=2, concat_axis=1, tiled=True)
    amount = portion.shape[3]
    flattened = portion.reshape(2, N2, block_a * amount)
    real_in = flattened[0]
    imag_in = flattened[1]
    real_mid = jnp.dot(cos_b, real_in, precision=highest) - jnp.dot(
        sin_b, imag_in, precision=highest
    )
    imag_mid = jnp.dot(sin_b, real_in, precision=highest) + jnp.dot(
        cos_b, imag_in, precision=highest
    )
    real_mid = real_mid.reshape(N2, block_a, amount)
    imag_mid = imag_mid.reshape(N2, block_a, amount)
    real_tw = real_mid * twid_cos[:, :, None] - imag_mid * twid_sin[:, :, None]
    imag_tw = real_mid * twid_sin[:, :, None] + imag_mid * twid_cos[:, :, None]
    spectra = jnp.stack([real_tw, imag_tw])
    regrouped = lax.all_to_all(spectra, "emit", split_axis=1, concat_axis=2, tiled=True)
    steps_a = jnp.arange(N1, dtype=jnp.int32)
    cos_a, sin_a = phases(steps_a[:, None] * steps_a[None, :] % N1, N1)
    real_full = jnp.einsum("ka,bar->bkr", cos_a, regrouped[0], precision=highest) - jnp.einsum(
        "ka,bar->bkr", sin_a, regrouped[1], precision=highest
    )
    imag_full = jnp.einsum("ka,bar->bkr", sin_a, regrouped[0], precision=highest) + jnp.einsum(
        "ka,bar->bkr", cos_a, regrouped[1], precision=highest
    )
    offset = freq_part - position * block_b
    is_owned = (offset >= 0) & (offset < block_b)
    flat_index = jnp.where(is_owned, offset, 0) * N1 + freq_high
    owned_mask = is_owned.astype(jnp.float32)[:, None]
    real_pick = (
        jnp.take(real_full.reshape(block_b * N1, rows_here), flat_index, axis=0) * owned_mask
    )
    imag_pick = (
        jnp.take(imag_full.reshape(block_b * N1, rows_here), flat_index, axis=0) * owned_mask
    )
    contribution = jnp.stack([real_pick, imag_pick], axis=1)
    raw_sketch = lax.psum_scatter(contribution, "emit", scatter_dimension=0, tiled=True)
    energy = jnp.sum(raw_sketch * raw_sketch, axis=(1, 2))
    column_total = lax.psum(energy, "panel")
    inverse_norm = lax.rsqrt(column_total / (rows_here * lax.axis_size("panel")) + 1e-06)
    return raw_sketch * inverse_norm[:, None, None]


def solution(mesh):
    placed = (P(None, "emit", "panel"), P("emit"), P())
    return jax.shard_map(
        body, mesh=mesh, in_specs=placed, out_specs=P("emit", None, "panel"), check_vma=False
    )
```

profile of v0, /device:TPU:1, one launch (start us, length us, event | category | flops | bytes accessed | tf_op | source)
XLA Modules:
  0.0 716.4 jit_solution(7302994786402832896)
XLA Ops:
  6.5 0.7 add_convert_fusion
  7.3 3.3 broadcast_multiply_fusion
  10.6 6.3 copy.50
  16.9 12.7 %all-to-all-start = ((f32[2,16,384,128]{3,1,0,2:T(8,128)}), f32[2,16,384,128]{3,1,0,2:T(8,128)}, u32[]{:S(2)}, u32[]{:S(2)}) async-start(f32[2,16,384,128]{3,1,0,2:T(8,128)} %copy.50), calls=%async_computation | async-start | bytes 12582912 | tf_op jit(solution)/shard_map/all_to_all | solution.py:33
  29.6 0.2 fusion.58
  29.8 137.7 %all-to-all-done = f32[2,16,384,128]{3,1,0,2:T(8,128)} async-done(((f32[2,16,384,128]{3,1,0,2:T(8,128)}), f32[2,16,384,128]{3,1,0,2:T(8,128)}, u32[]{:S(2)}, u32[]{:S(2)}) %all-to-all-start) | async-done | bytes 6291488 | tf_op jit(solution)/shard_map/all_to_all | solution.py:33
  167.5 3.3 copy.51
  170.8 0.7 fusion.93
  171.6 1.2 copy.52
  172.8 9.7 %fusion.4 = f32[512,1536]{1,0:T(8,128)S(1)} fusion(f32[64,8,12,128]{3,2,1,0:T(8,128)S(1)} %bitcast.60), kind=kOutput, calls=%fused_computation.9 | convolution fusion | flops 4835508224 | bytes 6291456 | tf_op jit(solution)/shard_map/dot_general | solution.py:38
  182.5 11.4 %fusion.2 = f32[512,1536]{1,0:T(8,128)} fusion(f32[64,8,12,128]{3,2,1,0:T(8,128)S(1)} %bitcast.61), kind=kOutput, calls=%fused_computation.7 | convolution fusion | flops 4835508224 | bytes 6291456 | tf_op jit(solution)/shard_map/dot_general | solution.py:41
  193.9 1.2 copy.53
  195.1 0.0 copy-start.1
  195.1 1.9 copy-done.1
  197.1 11.6 %convolution_subtract_fusion = f32[512,1536]{1,0:T(8,128)} fusion(f32[512,1536]{1,0:T(8,128)S(1)} %fusion.4, f32[64,8,12,128]{3,2,1,0:T(8,128)S(1)} %bitcast.51), kind=kOutput, calls=%fused_computation.4 | convolution fusion | flops 4836294656 | bytes 9437184 | tf_op jit(solution)/shard_map/dot_general | solution.py:38
  208.7 2.4 copy.54
  211.0 14.8 %convolution_add_fusion = f32[512,1536]{1,0:T(8,128)} fusion(f32[512,1536]{1,0:T(8,128)} %fusion.2, f32[64,8,12,128]{3,2,1,0:T(8,128)} %bitcast.52), kind=kOutput, calls=%fused_computation.3 | convolution fusion | flops 4836294656 | bytes 9437184 | tf_op jit(solution)/shard_map/dot_general | solution.py:41
  225.8 3.5 copy.55
  229.4 2.9 multiply_subtract_fusion
  232.2 3.4 pad_maximum_fusion
  235.6 10.4 %copy.56 = f32[2,512,12,128]{3,0,2,1:T(2,128)} copy(f32[2,512,12,128]{1,3,2,0:T(8,128)} %pad_maximum_fusion) | data formatting | bytes 12582912 | tf_op jit(solution)/shard_map/stack | solution.py:48
  246.0 11.7 %all-to-all-start.1 = ((f32[2,512,12,128]{3,0,2,1:T(2,128)}), f32[2,512,12,128]{3,0,2,1:T(2,128)}, u32[]{:S(2)}, u32[]{:S(2)}) async-start(f32[2,512,12,128]{3,0,2,1:T(2,128)} %copy.56), calls=%async_computation.1 | async-start | bytes 12582912 | tf_op jit(solution)/shard_map/all_to_all | solution.py:49
  257.8 0.0 reduce-scatter.2.cloned.1.call-start
  257.8 0.0 copy-done.4
  257.9 139.6 %all-to-all-done.1 = f32[2,512,12,128]{3,0,2,1:T(2,128)} async-done(((f32[2,512,12,128]{3,0,2,1:T(2,128)}), f32[2,512,12,128]{3,0,2,1:T(2,128)}, u32[]{:S(2)}, u32[]{:S(2)}) %all-to-all-start.1) | async-done | bytes 6291488 | tf_op jit(solution)/shard_map/all_to_all | solution.py:49
  397.4 4.0 copy.57
  401.4 2.4 fusion.92
  403.8 2.1 copy.58
  405.9 2.6 copy.59
  408.4 9.8 %fusion.20 = f32[16,128,384]{2,1,0:T(8,128)} fusion(f32[16,384,128]{1,2,0:T(8,128)S(1)} %copy.59), kind=kOutput, calls=%fused_computation.37 | convolution fusion | flops 3625205760 | bytes 6291456 | tf_op jit(solution)/shard_map/ka,bar->bkr/dot_general | solution.py:55
  418.2 9.9 %fusion.24 = f32[16,128,384]{2,1,0:T(8,128)} fusion(f32[16,384,128]{1,2,0:T(8,128)S(1)} %copy.59), kind=kOutput, calls=%fused_computation.41 | convolution fusion | flops 3625205760 | bytes 6291456 | tf_op jit(solution)/shard_map/ka,bar->bkr/dot_general | solution.py:52
  428.2 2.1 copy.60
  430.3 2.4 copy.61
  432.7 1.7 copy-done
  434.4 12.6 %add_bitcast_fusion = f32[16,384,128]{1,2,0:T(8,128)} fusion(f32[16,128,384]{2,1,0:T(8,128)} %fusion.20, f32[16,384,128]{1,2,0:T(8,128)S(1)} %copy.61), kind=kOutput, calls=%fused_computation.11 | convolution fusion | flops 3625992192 | bytes 9437184 | tf_op jit(solution)/shard_map/ka,bar->bkr/dot_general | solution.py:55
  446.9 2.4 copy.65
  449.3 13.8 %subtract_bitcast_fusion = f32[16,384,128]{1,2,0:T(8,128)} fusion(f32[16,128,384]{2,1,0:T(8,128)} %fusion.24, f32[16,384,128]{1,2,0:T(8,128)} %copy-done), kind=kOutput, calls=%fused_computation.12 | convolution fusion | flops 3625992192 | bytes 9437184 | tf_op jit(solution)/shard_map/ka,bar->bkr/dot_general | solution.py:52
  463.1 3.6 copy.62
  466.7 3.7 gather_fusion.1
  470.3 4.6 gather_fusion
  474.9 1.1 fusion.17
  476.0 1.2 pad_maximum_fusion.1
  477.3 0.0 reduce-scatter.2.cloned.1.call-update
  477.3 211.7 %reduce-scatter.2.cloned.1.call-done = f32[48,2,128]{2,0,1:T(8,128)} async-done(((f32[1536,2,128]{2,0,1:T(8,128)}), f32[48,2,128]{2,0,1:T(8,128)}) %reduce-scatter.2.cloned.1.call-update) | async-done | bytes 49168 | tf_op jit(solution)/shard_map/reduce_scatter | solution.py:69
  689.0 0.9 multiply_reduce_fusion
  689.9 17.8 %psum.7 = f32[48]{0:T(128)S(1)} all-reduce(f32[48]{0:T(128)S(1)} %multiply_reduce_fusion), channel_id=1, replica_groups=mesh['emit'=32,'panel'=8] {'panel'}, use_global_device_ids=true, to_apply=%region_2.4 | all-reduce | flops 48 | bytes 384 | tf_op jit(solution)/shard_map/psum | solution.py:71
  707.8 0.9 broadcast_multiply_fusion.1
  708.7 0.6 copy.66
  (10 shorter events, 0.1 us)
Async XLA Ops:
  16.9 150.6 %all-to-all-start = ((f32[2,16,384,128]{3,1,0,2:T(8,128)}), f32[2,16,384,128]{3,1,0,2:T(8,128)}, u32[]{:S(2)}, u32[]{:S(2)}) async-start(f32[2,16,384,128]{3,1,0,2:T(8,128)} %copy.50), calls=%async_computation | async-start | bytes 12582912 | tf_op jit(solution)/shard_map/all_to_all | solution.py:33
  195.1 1.9 copy-start.1
  246.0 11.8 %copy-start.4 = (s32[1536]{0:T(1024)S(1)}, s32[1536]{0:T(1024)}, u32[]{:S(2)}) copy-start(s32[1536]{0:T(1024)} %param.7) | copy-start | bytes 18436
  246.0 151.4 %all-to-all-start.1 = ((f32[2,512,12,128]{3,0,2,1:T(2,128)}), f32[2,512,12,128]{3,0,2,1:T(2,128)}, u32[]{:S(2)}, u32[]{:S(2)}) async-start(f32[2,512,12,128]{3,0,2,1:T(2,128)} %copy.56), calls=%async_computation.1 | async-start | bytes 12582912 | tf_op jit(solution)/shard_map/all_to_all | solution.py:49
  257.8 431.3 %reduce-scatter.2.cloned.1.call-start = ((), (), s32[]{:S(2)}) async-start(), calls=%async_computation.3 | async-start | bytes 1622016 | tf_op jit(solution)/shard_map/reduce_scatter | solution.py:69
  418.2 9.9 %copy-start.2 = (f32[1,16,32,12,128]{4,1,2,3,0:T(8,128)S(1)}, f32[1,16,32,12,128]{4,1,2,3,0:T(8,128)}, u32[]{:S(2)}) copy-start(f32[1,16,32,12,128]{4,1,2,3,0:T(8,128)} %get-tuple-element.10) | copy-start | bytes 9437188
  432.7 1.7 copy-start
  470.3 4.6 copy-start.3
Sparse Core Ops, SparseCore 0:
  477.4 211.5 reduce-scatter.1
where the time goes:
time: 721 us; the launch traced here: 716 us
  waiting for transfers between devices  489 us (68%)
  matrix products  93.6 us (13%)
  local copies, waits for them, and re-layouts  63 us (9%)
  starting transfers between devices  24.4 us (3%)
  blocking collectives  17.8 us (2%)
  other arithmetic  14.7 us (2%)
  between operations  13.9 us (2%)
    reduce_scatter x1, waiting for transfers between devices, body(): lax.psum_scatter(contribution, 'emit', scatter_dimension=0, tiled=True)  212 us
    all_to_all x1, waiting for transfers between devices, body(): lax.all_to_all(spectra, 'emit', split_axis=1, concat_axis=2, tiled=True)  140 us
    all_to_all x1, waiting for transfers between devices, body(): lax.all_to_all(blocked, 'emit', split_axis=2, concat_axis=1, tiled=True)  138 us
    psum x1, blocking collectives, body(): column_total = lax.psum(energy, 'panel')  17.8 us
    dot_general x1, matrix products, body(): jnp.dot(cos_b, imag_in, precision=highest)  14.8 us
  transfers between devices with their start and end apart: 3, of which 3 were waited for; matrix products, arithmetic and copies ran while one was open for 0% of the time, Pallas kernels for 0%

commit v1 on v0

v1 whole, which is shorter than its diff:
```python
import functools
import math

import jax
import jax.numpy as jnp
from jax import lax
from jax.experimental import pallas as pl
from jax.experimental.pallas import tpu as pltpu
from jax.sharding import PartitionSpec as P

EMITTERS = 196608
SKETCH = 1536
LOCAL = 6144
INNER = 8
HALF = 384
DEPTH = 2 * HALF
LANES = 128
PICK_ROWS = SKETCH // LANES
SIGN_ROWS = LOCAL // LANES
CHUNK = 384


def wrap(values, period):
    return values - period * jnp.round(values * (1.0 / period))


def cos_sin(residue, period):
    t = residue * (math.pi / (2.0 * period))
    s = t * t
    sin = t * (1.0 + s * (-1.0 / 6 + s * (1.0 / 120 + s * (-1.0 / 5040 + s * (1.0 / 362880)))))
    versin = s * (0.5 + s * (-1.0 / 24 + s * (1.0 / 720 + s * (-1.0 / 40320))))
    cos = 1.0 - versin
    sin, cos = 2.0 * sin * cos, 1.0 - 2.0 * sin * sin
    return 1.0 - 2.0 * sin * sin, 2.0 * sin * cos


def split(values):
    high = values.astype(jnp.bfloat16)
    return high, (values - high.astype(jnp.float32)).astype(jnp.bfloat16)


def local_kernel(x_hbm, sign_ref, pick_ref, out_ref, x, fold, rhs, lhs_h, lhs_l, kb, w, pre, pad, tr, acc, sems):
    position = lax.axis_index("emit")
    parts = 8
    rows = LOCAL // parts
    copies = []
    for part in range(parts):
        sl = pl.ds(part * rows, rows)
        copy = pltpu.make_async_copy(x_hbm.at[:, sl], x.at[:, sl], sems.at[part])
        copy.start()
        copies.append(copy)

    pad[...] = jnp.zeros_like(pad)
    k = pick_ref[...]
    kf = k.astype(jnp.float32)
    turn = 6144 * ((position * k) & 31) + 3068 * k
    turn = turn - EMITTERS * jnp.round(turn.astype(jnp.float32) * (1.0 / EMITTERS)).astype(jnp.int32)
    reduced = wrap(kf, 49152.0)
    w_cos, w_sin = cos_sin(wrap(kf, float(EMITTERS)), float(EMITTERS))
    p_cos, p_sin = cos_sin(turn.astype(jnp.float32), float(EMITTERS))
    r_cos, r_sin = cos_sin(wrap(reduced * 256.0, 49152.0), 49152.0)
    for slot, value in enumerate((reduced, w_cos, w_sin, p_cos, p_sin, r_cos, r_sin)):
        pad[slot * 16 : slot * 16 + PICK_ROWS] = value
    tr[0] = pad[...].T
    pad[0:SIGN_ROWS] = (2 * sign_ref[...] - 1).astype(jnp.float32)
    tr[1] = pad[...].T
    for q in range(PICK_ROWS):
        sl = slice(q * LANES, (q + 1) * LANES)

        def column(slot):
            c = slot * 16 + q
            return jnp.broadcast_to(tr[0, :, c : c + 1], (LANES, LANES))

        kb[0, sl] = column(0)
        w[0, sl] = column(1)
        w[1, sl] = column(2)
        pre[0, sl] = column(3)
        pre[1, sl] = column(4)
        kb[1, sl] = column(5)
        kb[2, sl] = column(6)

    odd = (2 * lax.broadcasted_iota(jnp.int32, (16, LANES), 1) + 1).astype(jnp.float32)

    @pl.loop(0, SKETCH // 16, unroll=2)
    def _(t):
        sl = pl.ds(pl.multiple_of(t * 16, 16), 16)
        cos, sin = cos_sin(wrap(kb[0, sl] * odd, 49152.0), 49152.0)
        r_cos = kb[1, sl]
        r_sin = kb[2, sl]
        for g in range(3):
            for base, value in ((0, cos), (HALF, sin)):
                high, low = split(value)
                lanes = slice(base + g * LANES, base + (g + 1) * LANES)
                lhs_h[sl, lanes] = high
                lhs_l[sl, lanes] = low
            if g < 2:
                cos, sin = cos * r_cos - sin * r_sin, sin * r_cos + cos * r_sin

    for copy in copies:
        copy.wait()

    for upper in range(SIGN_ROWS // 2, SIGN_ROWS):
        lower = SIGN_ROWS - 1 - upper
        sign_u = jnp.broadcast_to(tr[1, :, upper : upper + 1], (LANES, LANES))
        sign_l = jnp.broadcast_to(tr[1, :, lower : lower + 1], (LANES, LANES))
        for part in range(2):
            above = x[part, upper * LANES : (upper + 1) * LANES] * sign_u
            below = x[part, lower * LANES : (lower + 1) * LANES] * sign_l
            below = jnp.concatenate([below[8 * t : 8 * t + 8] for t in range(15, -1, -1)], axis=0)
            sl = slice((upper - SIGN_ROWS // 2) * LANES, (upper - SIGN_ROWS // 2 + 1) * LANES)
            fold[part, 0, sl] = above + below
            fold[part, 1, sl] = above - below

    @pl.loop(0, INNER)
    def _(i):
        pick = pl.ds(i, HALF, stride=INNER)
        quarters = (
            (fold[0, 0, pick], 0, 0),
            (fold[1, 0, pick], 0, LANES),
            (fold[1, 1, pick], HALF, 0),
            (-fold[0, 1, pick], HALF, LANES),
        )
        for value, row, lane in quarters:
            high, low = split(value)
            lanes = slice(lane, lane + LANES)
            rhs[i, row : row + HALF, lanes] = high
            rhs[i, DEPTH + row : DEPTH + row + HALF, lanes] = low
            rhs[i, 2 * DEPTH + row : 2 * DEPTH + row + HALF, lanes] = high

    @pl.loop(0, SKETCH // CHUNK)
    def _(c):
        sl = pl.ds(pl.multiple_of(c * CHUNK, CHUNK), CHUNK)
        acc[...] = jnp.zeros_like(acc)

        @pl.loop(0, INNER)
        def _(step):
            high = lhs_h[sl]
            lhs = jnp.concatenate([high, high, lhs_l[sl]], axis=1)
            y = jnp.dot(lhs, rhs[INNER - 1 - step], preferred_element_type=jnp.float32)
            real, imag = acc[:, :LANES], acc[:, LANES:]
            cos, sin = w[0, sl], w[1, sl]
            acc[:, :LANES] = real * cos + imag * sin + y[:, :LANES]
            acc[:, LANES:] = imag * cos - real * sin + y[:, LANES:]

        real, imag = acc[:, :LANES], acc[:, LANES:]
        cos, sin = pre[0, sl], pre[1, sl]
        out_ref[sl, :LANES] = real * cos + imag * sin
        out_ref[sl, LANES:] = imag * cos - real * sin


def local_sketch(green_matrix, sign_bits, column_picks):
    f32, bf16 = jnp.float32, jnp.bfloat16
    return pl.pallas_call(
        local_kernel,
        out_shape=jax.ShapeDtypeStruct((SKETCH, 2 * LANES), f32),
        in_specs=[
            pl.BlockSpec(memory_space=pl.ANY),
            pl.BlockSpec(memory_space=pltpu.VMEM),
            pl.BlockSpec(memory_space=pltpu.VMEM),
        ],
        out_specs=pl.BlockSpec(memory_space=pltpu.VMEM),
        scratch_shapes=[
            pltpu.VMEM((2, LOCAL, LANES), f32),
            pltpu.VMEM((2, 2, LOCAL // 2, LANES), f32),
            pltpu.VMEM((INNER, 3 * DEPTH, 2 * LANES), bf16),
            pltpu.VMEM((SKETCH, DEPTH), bf16),
            pltpu.VMEM((SKETCH, DEPTH), bf16),
            pltpu.VMEM((3, SKETCH, LANES), f32),
            pltpu.VMEM((2, SKETCH, LANES), f32),
            pltpu.VMEM((2, SKETCH, LANES), f32),
            pltpu.VMEM((LANES, LANES), f32),
            pltpu.VMEM((2, LANES, LANES), f32),
            pltpu.VMEM((CHUNK, 2 * LANES), f32),
            pltpu.SemaphoreType.DMA((8,)),
        ],
        compiler_params=pltpu.CompilerParams(vmem_limit_bytes=56 * 1024 * 1024),
    )(green_matrix, sign_bits.reshape(SIGN_ROWS, LANES), column_picks.reshape(PICK_ROWS, LANES))


def body(green_matrix, sign_bits, column_picks):
    partial = local_sketch(green_matrix, sign_bits, column_picks)
    raw_sketch = lax.psum_scatter(partial, "emit", scatter_dimension=0, tiled=True)
    energy = jnp.sum(raw_sketch * raw_sketch, axis=1)
    column_total = lax.psum(energy, "panel")
    inverse_norm = lax.rsqrt(column_total / (LANES * lax.axis_size("panel")) + 1e-06)
    return (raw_sketch * inverse_norm[:, None]).reshape(-1, 2, LANES)


def solution(mesh):
    placed = (P(None, "emit", "panel"), P("emit"), P())
    return jax.shard_map(
        body, mesh=mesh, in_specs=placed, out_specs=P("emit", None, "panel"), check_vma=False
    )
```

time: 721 us -> 278 us (0.39)
  waiting for transfers between devices: 489 us -> 214 us
  matrix products: 93.6 us -> 0 us
  local copies, waits for them, and re-layouts: 63 us -> 0.65 us
  Pallas kernels: 0 us -> 29.8 us
  starting transfers between devices: 24.4 us -> 0.01 us
  other arithmetic: 14.7 us -> 1.79 us
    all_to_all x2 -> x0, waiting for transfers between devices: 277 us -> none  [the longest x1 140 us: body(): lax.all_to_all(spectra, 'emit', split_axis=1, concat_axis=2, tiled=True)]
    dot_general x8 -> x0, matrix products: 93.6 us -> none  [the longest x1 14.8 us: body(): jnp.dot(cos_b, imag_in, precision=highest)]
    pallas_call x0 -> x1, Pallas kernels: none -> 29.8 us  [local_sketch(): pl.pallas_call(local_kernel, out_shape=jax.ShapeDtypeStruct((SKETCH, 2 *...]
    all_to_all x2 -> x0, starting transfers between devices: 24.4 us -> none  [the longest x1 12.7 us: body(): lax.all_to_all(blocked, 'emit', split_axis=2, concat_axis=1, tiled=True)]
    another operation x1 -> x0, local copies, waits for them, and re-layouts: 10.4 us -> none  [body(): spectra = jnp.stack([real_tw, imag_tw])]
    slice x6 -> x0, local copies, waits for them, and re-layouts: 9.75 us -> none  [the longest x2 4.47 us: body(): regrouped[1]]
    gather x2 -> x0, local copies, waits for them, and re-layouts: 8.22 us -> none  [the longest x1 4.55 us: body(): jnp.take(real_full.reshape(block_b * N1, rows_here), flat_index, axis=0)]
    all_to_all x2 -> x0, local copies, waits for them, and re-layouts: 7.28 us -> none  [the longest x1 4 us: body(): lax.all_to_all(spectra, 'emit', split_axis=1, concat_axis=2, tiled=True)]
  transfers between devices with their start and end apart: 3 -> 1, of which waited for: 3 -> 1; matrix products, arithmetic and copies ran while one was open for 0% -> 0% of each run, Pallas kernels for 0% -> 0%
where the time goes in v1:
time: 278 us; the launch traced here: 277 us
  waiting for transfers between devices  214 us (77%)
  Pallas kernels  29.8 us (11%)
  blocking collectives  17.8 us (6%)
  between operations  13.4 us (5%)
    reduce_scatter x1, waiting for transfers between devices, body(): lax.psum_scatter(partial, 'emit', scatter_dimension=0, tiled=True)  214 us
    pallas_call x1, Pallas kernels, local_sketch(): pl.pallas_call(local_kernel, out_shape=jax.ShapeDtypeStruct((SKETCH, 2 *...  29.8 us
    psum x1, blocking collectives, body(): column_total = lax.psum(energy, 'panel')  17.8 us
  transfers between devices with their start and end apart: 1, of which 1 were waited for; matrix products, arithmetic and copies ran while one was open for 0% of the time, Pallas kernels for 0%

profile of v1, /device:TPU:1, one launch (start us, length us, event | category | flops | bytes accessed | tf_op | source)
XLA Modules:
  0.0 277.2 jit_solution(7098365019012752823)
XLA Ops:
  6.5 0.0 reduce-scatter.2.cloned.1.call-start
  6.5 29.8 %shard_map.37 = f32[1536,256]{1,0:T(8,128)} custom-call(f32[2,6144,128]{2,1,0:T(8,128)} %x_hbm.1, s32[48,128]{1,0:T(8,128)} %bitcast.2, s32[12,128]{1,0:T(8,128)} %bitcast.3), custom_call_target="tpu_custom_call" | custom-call | tf_op jit(solution)/shard_map/pallas_call | solution.py:153
  36.4 0.0 reduce-scatter.2.cloned.1.call-update
  36.4 213.7 %reduce-scatter.2.cloned.1.call-done = f32[48,256]{1,0:T(8,128)} async-done(((f32[1536,256]{1,0:T(8,128)}), f32[48,256]{1,0:T(8,128)}) %reduce-scatter.2.cloned.1.call-update) | async-done | bytes 49168 | tf_op jit(solution)/shard_map/reduce_scatter | solution.py:182
  250.1 0.9 multiply_reduce_fusion
  251.0 17.8 %psum.7 = f32[48]{0:T(128)S(1)} all-reduce(f32[48]{0:T(128)S(1)} %multiply_reduce_fusion), channel_id=1, replica_groups=mesh['emit'=32,'panel'=8] {'panel'}, use_global_device_ids=true, to_apply=%region_2.0 | all-reduce | flops 48 | bytes 384 | tf_op jit(solution)/shard_map/psum | solution.py:184
  268.9 0.9 broadcast_multiply_fusion
  269.8 0.6 reshape.12
  (1 shorter events, 0.0 us)
Async XLA Ops:
  6.5 243.6 %reduce-scatter.2.cloned.1.call-start = ((), (), s32[]{:S(2)}) async-start(), calls=%async_computation.1 | async-start | bytes 1622016 | tf_op jit(solution)/shard_map/reduce_scatter | solution.py:182
Sparse Core Ops, SparseCore 0:
  36.5 213.5 reduce-scatter.1

commit v2 on v1

v2 whole, which is shorter than its diff:
```python
import math

import jax
import jax.numpy as jnp
from jax import lax
from jax.experimental import pallas as pl
from jax.experimental.pallas import tpu as pltpu
from jax.sharding import PartitionSpec as P

EMITTERS = 196608
SKETCH = 1536
LOCAL = 6144
INNER = 8
HALF = 384
DEPTH = 2 * HALF
LANES = 128
PICK_ROWS = SKETCH // LANES
SIGN_ROWS = LOCAL // LANES
RING_Z = 8
RING_Y = 4
PANELS = 8
OWN = SKETCH // (RING_Z * RING_Y)
BLOCK = OWN * RING_Y


MESH = pl.DeviceIdType.MESH


def wrap(values, period):
    return values - period * jnp.round(values * (1.0 / period))


def cos_sin(residue, period):
    t = residue * (math.pi / (2.0 * period))
    s = t * t
    sin = t * (1.0 + s * (-1.0 / 6 + s * (1.0 / 120 + s * (-1.0 / 5040 + s * (1.0 / 362880)))))
    versin = s * (0.5 + s * (-1.0 / 24 + s * (1.0 / 720 + s * (-1.0 / 40320))))
    cos = 1.0 - versin
    sin, cos = 2.0 * sin * cos, 1.0 - 2.0 * sin * sin
    return 1.0 - 2.0 * sin * sin, 2.0 * sin * cos


def split(values):
    high = values.astype(jnp.bfloat16)
    return high, (values - high.astype(jnp.float32)).astype(jnp.bfloat16)


def kernel(
    x_hbm, sign_ref, pick_ref, out_ref,
    x, fold, rhs_h, rhs_l, lhs_h, lhs_l, kb, w, pre, pad, tr, acc,
    z_out, z_in, y_in, energy, n_in,
    x_sem, z_send, z_recv, y_send, y_recv, n_send, n_recv,
):
    position = lax.axis_index("emit")
    panel = lax.axis_index("panel")
    y_here, z_here = position // RING_Z, position % RING_Z

    def at_z(d):
        return {"emit": y_here * RING_Z + (z_here + d) % RING_Z}

    def at_y(d):
        return {"emit": (y_here + d) % RING_Y * RING_Z + z_here}

    def at_panel(d):
        return {"panel": (panel + d) % PANELS}

    parts = 8
    rows = LOCAL // parts
    copies = []
    for part in range(parts):
        sl = pl.ds(part * rows, rows)
        copy = pltpu.make_async_copy(x_hbm.at[:, sl], x.at[:, sl], x_sem.at[part])
        copy.start()
        copies.append(copy)

    barrier = pltpu.get_barrier_semaphore()
    partners = [at_z(1), at_z(-1)]
    partners += [at_y(d) for d in range(1, RING_Y)]
    partners += [at_panel(d) for d in range(1, PANELS)]
    for partner in partners:
        pl.semaphore_signal(barrier, inc=1, device_id=partner, device_id_type=MESH)

    pad[...] = jnp.zeros_like(pad)
    k = pick_ref[...]
    kf = k.astype(jnp.float32)
    turn = 6144 * ((position * k) & 31) + 3068 * k
    turn = turn - EMITTERS * jnp.round(turn.astype(jnp.float32) * (1.0 / EMITTERS)).astype(jnp.int32)
    reduced = wrap(kf, 49152.0)
    w_cos, w_sin = cos_sin(wrap(kf, float(EMITTERS)), float(EMITTERS))
    p_cos, p_sin = cos_sin(turn.astype(jnp.float32), float(EMITTERS))
    r_cos, r_sin = cos_sin(wrap(reduced * 256.0, 49152.0), 49152.0)
    for slot, value in enumerate((reduced, w_cos, w_sin, p_cos, p_sin, r_cos, r_sin)):
        pad[slot * 16 : slot * 16 + PICK_ROWS] = value
    tr[0] = pad[...].T
    pad[0:SIGN_ROWS] = (2 * sign_ref[...] - 1).astype(jnp.float32)
    tr[1] = pad[...].T
    for q in range(PICK_ROWS):
        sl = slice(q * LANES, (q + 1) * LANES)
        for slot, ref in enumerate(
            (kb.at[0], w.at[0], w.at[1], pre.at[0], pre.at[1], kb.at[1], kb.at[2])
        ):
            c = slot * 16 + q
            ref[sl] = jnp.broadcast_to(tr[0, :, c : c + 1], (LANES, LANES))

    odd = (2 * lax.broadcasted_iota(jnp.int32, (16, LANES), 1) + 1).astype(jnp.float32)

    @pl.loop(0, SKETCH // 16)
    def _(t):
        sl = pl.ds(pl.multiple_of(t * 16, 16), 16)
        cos, sin = cos_sin(wrap(kb[0, sl] * odd, 49152.0), 49152.0)
        r_cos, r_sin = kb[1, sl], kb[2, sl]
        for g in range(3):
            if g:
                cos, sin = cos * r_cos - sin * r_sin, sin * r_cos + cos * r_sin
            for base, value in ((0, cos), (HALF, sin)):
                high, low = split(value)
                lanes = slice(base + g * LANES, base + (g + 1) * LANES)
                lhs_h[sl, lanes] = high
                lhs_l[sl, lanes] = low

    for copy in copies:
        copy.wait()

    for upper in range(SIGN_ROWS // 2, SIGN_ROWS):
        lower = SIGN_ROWS - 1 - upper
        sign_u = jnp.broadcast_to(tr[1, :, upper : upper + 1], (LANES, LANES))
        sign_l = jnp.broadcast_to(tr[1, :, lower : lower + 1], (LANES, LANES))
        sl = slice((upper - SIGN_ROWS // 2) * LANES, (upper - SIGN_ROWS // 2 + 1) * LANES)
        for part in range(2):
            above = x[part, upper * LANES : (upper + 1) * LANES] * sign_u
            below = x[part, lower * LANES : (lower + 1) * LANES] * sign_l
            below = jnp.concatenate([below[8 * t : 8 * t + 8] for t in range(15, -1, -1)], axis=0)
            fold[part, 0, sl] = above + below
            fold[part, 1, sl] = above - below

    @pl.loop(0, INNER)
    def _(i):
        pick = pl.ds(i, HALF, stride=INNER)
        quarters = (
            (fold[0, 0, pick], 0, 0),
            (fold[1, 0, pick], 0, LANES),
            (fold[1, 1, pick], HALF, 0),
            (-fold[0, 1, pick], HALF, LANES),
        )
        for value, row, lane in quarters:
            high, low = split(value)
            lanes = slice(lane, lane + LANES)
            rhs_h[i, row : row + HALF, lanes] = high
            rhs_l[i, row : row + HALF, lanes] = low

    def group(targets):
        slices = []
        for d, _ in targets:
            block = (z_here + d) % RING_Z
            slices.append(pl.ds(pl.multiple_of(block * BLOCK, BLOCK), BLOCK))
        for step in range(INNER):
            i = INNER - 1 - step
            high = jnp.concatenate([lhs_h[sl] for sl in slices], axis=0)
            low = jnp.concatenate([lhs_l[sl] for sl in slices], axis=0)
            lhs = jnp.concatenate([high, high, low], axis=1)
            xh = rhs_h[i]
            both = jnp.concatenate([xh, rhs_l[i], xh], axis=0)
            product = jnp.dot(lhs, both, preferred_element_type=jnp.float32)
            for n, sl in enumerate(slices):
                mine = slice(n * BLOCK, (n + 1) * BLOCK)
                new_real, new_imag = product[mine, :LANES], product[mine, LANES:]
                if step:
                    real, imag = acc[mine, :LANES], acc[mine, LANES:]
                    cos, sin = w[0, sl], w[1, sl]
                    new_real = real * cos + imag * sin + new_real
                    new_imag = imag * cos - real * sin + new_imag
                if i:
                    acc[mine, :LANES] = new_real
                    acc[mine, LANES:] = new_imag
                else:
                    cos, sin = pre[0, sl], pre[1, sl]
                    ref = targets[n][1]
                    ref[:, :LANES] = new_real * cos + new_imag * sin
                    ref[:, LANES:] = new_imag * cos - new_real * sin

    def z_copy(way, step, part=slice(None)):
        return pltpu.make_async_remote_copy(
            src_ref=z_out.at[way, step, part],
            dst_ref=z_in.at[way, step, part],
            send_sem=z_send.at[way, step],
            recv_sem=z_recv.at[way, step],
            device_id=at_z(1 - 2 * way),
            device_id_type=MESH,
        )

    half = BLOCK // 2
    halves = (pl.ds(0, half), pl.ds(half, half))
    group([(4, z_out.at[0, 0])])
    z_out[1, 0, half:] = z_out[0, 0, half:]
    pl.semaphore_wait(barrier, len(partners))
    sent = [z_copy(way, 0, halves[way]) for way in range(2)]
    for copy in sent:
        copy.start()
    last = sent
    for step in range(1, 4):
        group([(4 - step, z_out.at[0, step]), (step - 4, z_out.at[1, step])])
        copies = []
        for way in range(2):
            last[way].wait_recv()
            part = halves[way] if step == 1 else slice(None)
            z_out[way, step, part] += z_in[way, step - 1, part]
            copies.append(z_copy(way, step))
            copies[way].start()
        last = copies
        sent = sent + copies
    group([(0, acc.at[:BLOCK])])
    for way in range(2):
        last[way].wait_recv()
        acc[:BLOCK] += z_in[way, 3]

    copies = []
    for d in range(1, RING_Y):
        block = (y_here + d) % RING_Y
        copy = pltpu.make_async_remote_copy(
            src_ref=acc.at[pl.ds(pl.multiple_of(block * OWN, OWN), OWN)],
            dst_ref=y_in.at[d - 1],
            send_sem=y_send.at[d - 1],
            recv_sem=y_recv.at[d - 1],
            device_id=at_y(d),
            device_id_type=MESH,
        )
        copy.start()
        copies.append(copy)
    sent = sent + copies
    raw = acc[pl.ds(pl.multiple_of(y_here * OWN, OWN), OWN)]
    for d, copy in enumerate(copies):
        copy.wait_recv()
        raw = raw + y_in[d]

    real, imag = raw[:, :LANES], raw[:, LANES:]
    pad[...] = jnp.zeros_like(pad)
    pad[:OWN] = real * real + imag * imag
    total = jnp.sum(pad[...].T, axis=0, keepdims=True)
    energy[...] = jnp.broadcast_to(total, energy.shape)
    copies = []
    for d in range(1, PANELS):
        copy = pltpu.make_async_remote_copy(
            src_ref=energy,
            dst_ref=n_in.at[d - 1],
            send_sem=n_send.at[d - 1],
            recv_sem=n_recv.at[d - 1],
            device_id=at_panel(d),
            device_id_type=MESH,
        )
        copy.start()
        copies.append(copy)
    sent = sent + copies
    for d, copy in enumerate(copies):
        copy.wait_recv()
        total = total + n_in[d, :1]
    scale = lax.rsqrt(total * (1.0 / (LANES * PANELS)) + 1e-06)
    scale = jnp.broadcast_to(scale, (LANES, LANES)).T[:OWN]
    out_ref[:, :LANES] = real * scale
    out_ref[:, LANES:] = imag * scale
    for copy in sent:
        copy.wait_send()


def fused(green_matrix, sign_bits, picks):
    f32, bf16 = jnp.float32, jnp.bfloat16
    wide = 2 * LANES
    return pl.pallas_call(
        kernel,
        out_shape=jax.ShapeDtypeStruct((OWN, wide), f32),
        in_specs=[
            pl.BlockSpec(memory_space=pl.ANY),
            pl.BlockSpec(memory_space=pltpu.VMEM),
            pl.BlockSpec(memory_space=pltpu.VMEM),
        ],
        out_specs=pl.BlockSpec(memory_space=pltpu.VMEM),
        scratch_shapes=[
            pltpu.VMEM((2, LOCAL, LANES), f32),
            pltpu.VMEM((2, 2, LOCAL // 2, LANES), f32),
            pltpu.VMEM((INNER, DEPTH, wide), bf16),
            pltpu.VMEM((INNER, DEPTH, wide), bf16),
            pltpu.VMEM((SKETCH, DEPTH), bf16),
            pltpu.VMEM((SKETCH, DEPTH), bf16),
            pltpu.VMEM((3, SKETCH, LANES), f32),
            pltpu.VMEM((2, SKETCH, LANES), f32),
            pltpu.VMEM((2, SKETCH, LANES), f32),
            pltpu.VMEM((LANES, LANES), f32),
            pltpu.VMEM((2, LANES, LANES), f32),
            pltpu.VMEM((2 * BLOCK, wide), f32),
            pltpu.VMEM((2, 4, BLOCK, wide), f32),
            pltpu.VMEM((2, 4, BLOCK, wide), f32),
            pltpu.VMEM((RING_Y - 1, OWN, wide), f32),
            pltpu.VMEM((8, LANES), f32),
            pltpu.VMEM((PANELS - 1, 8, LANES), f32),
            pltpu.SemaphoreType.DMA((8,)),
            pltpu.SemaphoreType.DMA((2, 4)),
            pltpu.SemaphoreType.DMA((2, 4)),
            pltpu.SemaphoreType.DMA((RING_Y - 1,)),
            pltpu.SemaphoreType.DMA((RING_Y - 1,)),
            pltpu.SemaphoreType.DMA((PANELS - 1,)),
            pltpu.SemaphoreType.DMA((PANELS - 1,)),
        ],
        compiler_params=pltpu.CompilerParams(
            collective_id=0, has_side_effects=True, vmem_limit_bytes=56 * 1024 * 1024
        ),
    )(green_matrix, sign_bits, picks)


def body(green_matrix, sign_bits, column_picks):
    picks = column_picks.reshape(RING_Y, RING_Z, OWN).transpose(1, 0, 2).reshape(PICK_ROWS, LANES)
    sketch = fused(green_matrix, sign_bits.reshape(SIGN_ROWS, LANES), picks)
    return sketch.reshape(OWN, 2, LANES)


def solution(mesh):
    placed = (P(None, "emit", "panel"), P("emit"), P())
    return jax.shard_map(
        body, mesh=mesh, in_specs=placed, out_specs=P("emit", None, "panel"), check_vma=False
    )
```

time: 278 us -> 52 us (0.19)
  waiting for transfers between devices: 214 us -> 0 us
  Pallas kernels: 29.8 us -> 48.8 us
  blocking collectives: 17.8 us -> 0 us
  between operations: 13.4 us -> 0.02 us
    reduce_scatter x1 -> x0, waiting for transfers between devices: 214 us -> none  [body(): lax.psum_scatter(partial, 'emit', scatter_dimension=0, tiled=True)]
    pallas_call x1, Pallas kernels: 29.8 us -> 48.8 us  [fused(): pl.pallas_call(kernel, out_shape=jax.ShapeDtypeStruct((OWN, wide), f32),...]
    psum x1 -> x0, blocking collectives: 17.8 us -> none  [body(): column_total = lax.psum(energy, 'panel')]
  transfers between devices with their start and end apart: 1 -> 0, of which waited for: 1 -> 0; matrix products, arithmetic and copies ran while one was open for 0% -> 0% of each run, Pallas kernels for 0% -> 0%
where the time goes in v2:
time: 52 us; the launch traced here: 51.8 us
  Pallas kernels  48.8 us (94%)
  local copies, waits for them, and re-layouts  2.9 us (6%)
    pallas_call x1, Pallas kernels, fused(): pl.pallas_call(kernel, out_shape=jax.ShapeDtypeStruct((OWN, wide), f32),...  48.8 us
    reshape x2, local copies, waits for them, and re-layouts, body(): column_picks.reshape(RING_Y, RING_Z, OWN).transpose(1, 0, 2)  1.45 us
    reshape x1, local copies, waits for them, and re-layouts, body(): return sketch.reshape(OWN, 2, LANES)  1.44 us

profile of v2, /device:TPU:1, one launch (start us, length us, event | category | flops | bytes accessed | tf_op | source)
XLA Modules:
  0.0 51.8 jit_solution(6052723986195510827)
XLA Ops:
  0.0 0.8 %reshape.13 = s32[4,8,48]{2,1,0:T(8,128)S(1)} reshape(s32[1536]{0:T(1024)} %param.5) | data formatting | bytes 12288 | tf_op jit(solution)/shard_map/reshape | solution.py:309
  0.8 0.7 %reshape.14.pick_ref = s32[12,128]{1,0:T(8,128)} reshape(s32[8,4,48]{2,1,0:T(4,128)S(1)} %copy.4) | data formatting | bytes 12288 | tf_op jit(solution)/shard_map/reshape | solution.py:309
  1.5 48.8 %shard_map.37 = f32[48,256]{1,0:T(8,128)} custom-call(f32[2,6144,128]{2,1,0:T(8,128)} %x_hbm.1, s32[48,128]{1,0:T(8,128)} %bitcast.3, s32[12,128]{1,0:T(8,128)} %reshape.14.pick_ref), custom_call_target="tpu_custom_call" | custom-call | tf_op jit(solution)/shard_map/pallas_call | solution.py:267
  50.3 1.4 %reshape.15 = f32[48,2,128]{2,1,0:T(2,128)} reshape(f32[48,256]{1,0:T(8,128)} %shard_map.37) | data formatting | bytes 98304 | tf_op jit(solution)/shard_map/reshape | solution.py:311
  (1 shorter events, 0.0 us)

commit v3 on v2

v3 whole, which is shorter than its diff:
```python
import math

import jax
import jax.numpy as jnp
from jax import lax
from jax.experimental import pallas as pl
from jax.experimental.pallas import tpu as pltpu
from jax.sharding import PartitionSpec as P

EMITTERS = 196608
SKETCH = 1536
LOCAL = 6144
INNER = 8
HALF = 384
DEPTH = 2 * HALF
LANES = 128
PICK_ROWS = SKETCH // LANES
SIGN_ROWS = LOCAL // LANES
RING_Z = 8
RING_Y = 4
PANELS = 8
OWN = SKETCH // (RING_Z * RING_Y)
PART = OWN // 2
BLOCK_A = PART * RING_Y
BLOCK_B = PART * RING_Z
START_B = BLOCK_A * RING_Z
TILE = 32
FINE = jnp.float8_e4m3fn
STEP = 512.0
GROUPS = (
    (("a", 3), ("a", -3), ("b", 2)),
    (("a", 4), ("b", 1)),
    (("a", 1), ("a", -1), ("b", -1)),
    (("a", 2), ("a", -2)),
    (("b", 0), ("a", 0)),
)


MESH = pl.DeviceIdType.MESH


def wrap(values, period):
    return values - period * jnp.round(values * (1.0 / period))


def cos_sin(residue, period):
    t = residue * (math.pi / (2.0 * period))
    s = t * t
    sin = t * (1.0 + s * (-1.0 / 6 + s * (1.0 / 120 + s * (-1.0 / 5040 + s * (1.0 / 362880)))))
    versin = s * (0.5 + s * (-1.0 / 24 + s * (1.0 / 720 + s * (-1.0 / 40320))))
    cos = 1.0 - versin
    sin, cos = 2.0 * sin * cos, 1.0 - 2.0 * sin * sin
    return 1.0 - 2.0 * sin * sin, 2.0 * sin * cos


def table_row(column):
    owner, rest = divmod(column, OWN)
    y, z = divmod(owner, RING_Z)
    if rest < PART:
        return z * BLOCK_A + y * PART + rest
    return START_B + y * BLOCK_B + z * PART + rest - PART


def size(half):
    return BLOCK_A if half == "a" else BLOCK_B


def rows_before(group):
    return sum(size(half) for blocks in GROUPS[:group] for half, _ in blocks)


def kernel(
    x_hbm, sign_ref, pick_ref, out_ref,
    x, fold, rhs_h, rhs_l, lhs_h, lhs_l, kb, w, pre, pad, tr, acc, sum_a, sum_b,
    a_out, a_in, ya_in, b_out, b_in, zb_in, energy, n_in,
    x_sem, a_send, a_recv, ya_send, ya_recv, b_send, b_recv, zb_send, zb_recv, n_send, n_recv,
):
    position = lax.axis_index("emit")
    panel = lax.axis_index("panel")
    y_here, z_here = position // RING_Z, position % RING_Z

    def at_z(d):
        return {"emit": y_here * RING_Z + (z_here + d) % RING_Z}

    def at_y(d):
        return {"emit": (y_here + d) % RING_Y * RING_Z + z_here}

    def at_panel(d):
        return {"panel": (panel + d) % PANELS}

    parts = 8
    rows = LOCAL // parts
    copies = {}
    for part in (3, 4, 2, 5, 1, 6, 0, 7):
        sl = pl.ds(part * rows, rows)
        copies[part] = pltpu.make_async_copy(x_hbm.at[:, sl], x.at[:, sl], x_sem.at[part])
        copies[part].start()

    barrier = pltpu.get_barrier_semaphore()
    partners = [at_z(d) for d in range(1, RING_Z)]
    partners += [at_y(d) for d in range(1, RING_Y)]
    partners += [at_panel(d) for d in range(1, PANELS)]
    for partner in partners:
        pl.semaphore_signal(barrier, inc=1, device_id=partner, device_id_type=MESH)

    pad[...] = jnp.zeros_like(pad)
    k = pick_ref[...].reshape(PICK_ROWS, LANES)
    kf = k.astype(jnp.float32)
    turn = 6144 * ((position * k) & 31) + 3068 * k
    turn = turn - EMITTERS * jnp.round(turn.astype(jnp.float32) * (1.0 / EMITTERS)).astype(jnp.int32)
    reduced = wrap(kf, 49152.0)
    w_cos, w_sin = cos_sin(wrap(kf, float(EMITTERS)), float(EMITTERS))
    p_cos, p_sin = cos_sin(turn.astype(jnp.float32), float(EMITTERS))
    r_cos, r_sin = cos_sin(wrap(reduced * 256.0, 49152.0), 49152.0)
    for slot, value in enumerate((reduced, w_cos, w_sin, p_cos, p_sin, r_cos, r_sin)):
        pad[slot * 16 : slot * 16 + PICK_ROWS] = value
    tr[0] = pad[...].T
    pad[0:SIGN_ROWS] = (2 * sign_ref[...].reshape(SIGN_ROWS, LANES) - 1).astype(jnp.float32)
    tr[1] = pad[...].T
    for q in range(PICK_ROWS):
        for slot, ref in enumerate(
            (kb.at[0], w.at[0], w.at[1], pre.at[0], pre.at[1], kb.at[1], kb.at[2])
        ):
            c = slot * 16 + q
            spread = jnp.broadcast_to(tr[0, :, c : c + 1], (LANES, LANES))
            for first in range(0, LANES, 8):
                row = table_row(q * LANES + first)
                ref[row : row + 8] = spread[first : first + 8]

    odd = (2 * lax.broadcasted_iota(jnp.int32, (TILE, LANES), 1) + 1).astype(jnp.float32)

    def source(half, d):
        if half == "a":
            return pl.multiple_of((z_here + d) % RING_Z * BLOCK_A, TILE)
        return pl.multiple_of(START_B + (y_here + d) % RING_Y * BLOCK_B, TILE)

    def table_tile(first, row):
        sl = pl.ds(first, TILE)
        to = pl.ds(row, TILE)
        cos, sin = cos_sin(wrap(kb[0, sl] * odd, 49152.0), 49152.0)
        r_cos, r_sin = kb[1, sl], kb[2, sl]
        for g in range(3):
            if g:
                cos, sin = cos * r_cos - sin * r_sin, sin * r_cos + cos * r_sin
            for base, value in ((0, cos), (HALF, sin)):
                high = value.astype(jnp.bfloat16)
                lane = base + g * LANES
                lhs_h[to, lane : lane + LANES] = high
                lhs_l[to, lane : lane + LANES] = value.astype(FINE)
                rest = (value - high.astype(jnp.float32)) * STEP
                lhs_l[to, DEPTH + lane : DEPTH + lane + LANES] = rest.astype(FINE)

    row = 0
    for half, d in GROUPS[0]:
        first = source(half, d)

        @pl.loop(0, size(half) // TILE)
        def _(t, first=first, row=row):
            table_tile(
                pl.multiple_of(first + t * TILE, TILE), pl.multiple_of(row + t * TILE, TILE)
            )

        row += size(half)

    peak = jnp.zeros((LANES, LANES), jnp.float32)
    for upper in range(SIGN_ROWS // 2, SIGN_ROWS):
        lower = SIGN_ROWS - 1 - upper
        if upper * LANES % rows == 0:
            copies[upper * LANES // rows].wait()
            copies[lower * LANES // rows].wait()
        sign_u = jnp.broadcast_to(tr[1, :, upper : upper + 1], (LANES, LANES))
        sign_l = jnp.broadcast_to(tr[1, :, lower : lower + 1], (LANES, LANES))
        sl = slice((upper - SIGN_ROWS // 2) * LANES, (upper - SIGN_ROWS // 2 + 1) * LANES)
        for part in range(2):
            above = x[part, upper * LANES : (upper + 1) * LANES] * sign_u
            below = x[part, lower * LANES : (lower + 1) * LANES] * sign_l
            below = jnp.concatenate([below[8 * t : 8 * t + 8] for t in range(15, -1, -1)], axis=0)
            fold[part, 0, sl] = above + below
            fold[part, 1, sl] = above - below
            peak = jnp.maximum(peak, jnp.maximum(jnp.abs(above), jnp.abs(below)))
    peak = jnp.maximum(jnp.max(peak, axis=0, keepdims=True), 1e-30)
    scale = 65536.0 / peak
    unscale = peak * (1.0 / 65536.0)

    def convert(i):
        pick = pl.ds(i, HALF, stride=INNER)
        quarters = (
            (fold[0, 0, pick] * scale, 0, 0),
            (fold[1, 0, pick] * scale, 0, LANES),
            (fold[1, 1, pick] * scale, HALF, 0),
            (fold[0, 1, pick] * -scale, HALF, LANES),
        )
        for value, row, lane in quarters:
            high = value.astype(jnp.bfloat16)
            lanes = slice(lane, lane + LANES)
            rhs_h[i, row : row + HALF, lanes] = high
            rhs_l[i, row : row + HALF, lanes] = (value - high.astype(jnp.float32)).astype(FINE)
            rhs_l[i, DEPTH + row : DEPTH + row + HALF, lanes] = (value * (1.0 / STEP)).astype(FINE)

    convert(INNER - 1)

    def work(group, refs):
        blocks = GROUPS[group]
        start = rows_before(group)
        count = sum(size(half) for half, _ in blocks)
        tiles = []
        if group + 1 < len(GROUPS):
            row = start + count
            for half, d in GROUPS[group + 1]:
                first = source(half, d)
                for t in range(0, size(half), TILE):
                    tiles.append((pl.multiple_of(first + t, TILE), row + t))
                row += size(half)
        for step in range(INNER):
            i = INNER - 1 - step
            product = jnp.dot(
                lhs_h[start : start + count], rhs_h[i], preferred_element_type=jnp.float32
            ) + jnp.dot(
                lhs_l[start : start + count], rhs_l[i], preferred_element_type=jnp.float32
            )
            if group == 0 and i:
                convert(i - 1)
            for first, row in tiles[len(tiles) * step // INNER : len(tiles) * (step + 1) // INNER]:
                table_tile(first, row)
            first = 0
            for (half, d), ref in zip(blocks, refs):
                mine = slice(first, first + size(half))
                first += size(half)
                sl = pl.ds(source(half, d), size(half))
                new_real, new_imag = product[mine, :LANES], product[mine, LANES:]
                if step:
                    real, imag = acc[mine, :LANES], acc[mine, LANES:]
                    cos, sin = w[0, sl], w[1, sl]
                    new_real = real * cos + imag * sin + new_real
                    new_imag = imag * cos - real * sin + new_imag
                if i:
                    acc[mine, :LANES] = new_real
                    acc[mine, LANES:] = new_imag
                else:
                    cos, sin = pre[0, sl], pre[1, sl]
                    ref[:, :LANES] = (new_real * cos + new_imag * sin) * unscale
                    ref[:, LANES:] = (new_imag * cos - new_real * sin) * unscale

    sent = []

    def send(src, dst, sems, device):
        copy = pltpu.make_async_remote_copy(
            src_ref=src, dst_ref=dst, send_sem=sems[0], recv_sem=sems[1],
            device_id=device, device_id_type=MESH,
        )
        copy.start()
        sent.append(copy)
        return copy

    first_half = pl.ds(0, BLOCK_A // 2)
    second_half = pl.ds(BLOCK_A // 2, BLOCK_A // 2)
    whole = slice(None)

    def send_a(slot, out, to, part=whole):
        return send(
            a_out.at[out, part], a_in.at[slot, part], (a_send.at[slot], a_recv.at[slot]), at_z(to)
        )

    def send_b(d):
        slot = d % RING_Y - 1
        return send(b_out.at[slot], b_in.at[slot], (b_send.at[slot], b_recv.at[slot]), at_y(d))

    work(0, [a_out.at[0], a_out.at[1], b_out.at[1]])
    pl.semaphore_wait(barrier, len(partners))
    near = [send_a(0, 0, 1), send_a(1, 1, -1)]
    last_b = [send_b(2)]
    work(1, [a_out.at[2], b_out.at[0]])
    far = [send_a(2, 2, 2, first_half), send_a(3, 2, -2, second_half)]
    last_b.append(send_b(1))
    work(2, [a_out.at[3], a_out.at[4], b_out.at[2]])
    last_a = [send_a(4, 3, 1), send_a(5, 4, -1)]
    last_b.append(send_b(-1))
    work(3, [a_out.at[5], a_out.at[6]])
    for way, part in enumerate((first_half, second_half)):
        near[way].wait_recv()
        a_out[5 + way] += a_in[way]
        far[way].wait_recv()
        a_out[5 + way, part] += a_in[2 + way, part]
        last_a.append(send_a(6 + way, 5 + way, 2 - 4 * way))
    work(4, [sum_b, sum_a])

    def own(ref, place):
        return ref.at[pl.ds(pl.multiple_of(place * PART, PART), PART)]

    for copy in last_b:
        copy.wait_recv()
    sum_b[...] += b_in[0] + b_in[1] + b_in[2]
    copies_b = [
        send(
            own(sum_b, (z_here + d) % RING_Z), zb_in.at[d - 1],
            (zb_send.at[d - 1], zb_recv.at[d - 1]), at_z(d),
        )
        for d in range(1, RING_Z)
    ]
    for copy in last_a:
        copy.wait_recv()
    sum_a[...] += (a_in[4] + a_in[5]) + (a_in[6] + a_in[7])
    copies_a = [
        send(
            own(sum_a, (y_here + d) % RING_Y), ya_in.at[d - 1],
            (ya_send.at[d - 1], ya_recv.at[d - 1]), at_y(d),
        )
        for d in range(1, RING_Y)
    ]
    raw_b = own(sum_b, z_here)[...]
    for d, copy in enumerate(copies_b):
        copy.wait_recv()
        raw_b = raw_b + zb_in[d]
    raw_a = own(sum_a, y_here)[...]
    for d, copy in enumerate(copies_a):
        copy.wait_recv()
        raw_a = raw_a + ya_in[d]
    raw = jnp.concatenate([raw_a, raw_b], axis=0)

    real, imag = raw[:, :LANES], raw[:, LANES:]
    pad[...] = jnp.zeros_like(pad)
    pad[:OWN] = real * real + imag * imag
    total = jnp.sum(pad[...].T, axis=0, keepdims=True)
    energy[...] = jnp.broadcast_to(total, energy.shape)
    copies = [
        send(energy, n_in.at[d - 1], (n_send.at[d - 1], n_recv.at[d - 1]), at_panel(d))
        for d in range(1, PANELS)
    ]
    for d, copy in enumerate(copies):
        copy.wait_recv()
        total = total + n_in[d, :1]
    scale = lax.rsqrt(total * (1.0 / (LANES * PANELS)) + 1e-06)
    scale = jnp.broadcast_to(scale, (LANES, LANES)).T[:OWN]
    out_ref[:, 0] = real * scale
    out_ref[:, 1] = imag * scale
    for copy in sent:
        copy.wait_send()


def fused(green_matrix, sign_bits, picks):
    f32, bf16 = jnp.float32, jnp.bfloat16
    wide = 2 * LANES
    return pl.pallas_call(
        kernel,
        out_shape=jax.ShapeDtypeStruct((OWN, 2, LANES), f32),
        in_specs=[
            pl.BlockSpec(memory_space=pl.ANY),
            pl.BlockSpec(memory_space=pltpu.VMEM),
            pl.BlockSpec(memory_space=pltpu.VMEM),
        ],
        out_specs=pl.BlockSpec(memory_space=pltpu.VMEM),
        scratch_shapes=[
            pltpu.VMEM((2, LOCAL, LANES), f32),
            pltpu.VMEM((2, 2, LOCAL // 2, LANES), f32),
            pltpu.VMEM((INNER, DEPTH, wide), bf16),
            pltpu.VMEM((INNER, 2 * DEPTH, wide), FINE),
            pltpu.VMEM((SKETCH, DEPTH), bf16),
            pltpu.VMEM((SKETCH, 2 * DEPTH), FINE),
            pltpu.VMEM((3, SKETCH, LANES), f32),
            pltpu.VMEM((2, SKETCH, LANES), f32),
            pltpu.VMEM((2, SKETCH, LANES), f32),
            pltpu.VMEM((LANES, LANES), f32),
            pltpu.VMEM((2, LANES, LANES), f32),
            pltpu.VMEM((2 * BLOCK_A + BLOCK_B, wide), f32),
            pltpu.VMEM((BLOCK_A, wide), f32),
            pltpu.VMEM((BLOCK_B, wide), f32),
            pltpu.VMEM((7, BLOCK_A, wide), f32),
            pltpu.VMEM((8, BLOCK_A, wide), f32),
            pltpu.VMEM((RING_Y - 1, PART, wide), f32),
            pltpu.VMEM((RING_Y - 1, BLOCK_B, wide), f32),
            pltpu.VMEM((RING_Y - 1, BLOCK_B, wide), f32),
            pltpu.VMEM((RING_Z - 1, PART, wide), f32),
            pltpu.VMEM((8, LANES), f32),
            pltpu.VMEM((PANELS - 1, 8, LANES), f32),
            pltpu.SemaphoreType.DMA((8,)),
            pltpu.SemaphoreType.DMA((8,)),
            pltpu.SemaphoreType.DMA((8,)),
            pltpu.SemaphoreType.DMA((RING_Y - 1,)),
            pltpu.SemaphoreType.DMA((RING_Y - 1,)),
            pltpu.SemaphoreType.DMA((RING_Y - 1,)),
            pltpu.SemaphoreType.DMA((RING_Y - 1,)),
            pltpu.SemaphoreType.DMA((RING_Z - 1,)),
            pltpu.SemaphoreType.DMA((RING_Z - 1,)),
            pltpu.SemaphoreType.DMA((PANELS - 1,)),
            pltpu.SemaphoreType.DMA((PANELS - 1,)),
        ],
        compiler_params=pltpu.CompilerParams(
            collective_id=0, has_side_effects=True, vmem_limit_bytes=56 * 1024 * 1024
        ),
    )(green_matrix, sign_bits, picks)


def body(green_matrix, sign_bits, column_picks):
    return fused(green_matrix, sign_bits, column_picks)


def solution(mesh):
    placed = (P(None, "emit", "panel"), P("emit"), P())
    return jax.shard_map(
        body, mesh=mesh, in_specs=placed, out_specs=P("emit", None, "panel"), check_vma=False
    )
```

time: 52 us -> 42 us (0.81)
  Pallas kernels: 48.8 us -> 40.4 us
  local copies, waits for them, and re-layouts: 2.9 us -> 1.42 us
    pallas_call x1, Pallas kernels: 48.8 us -> 40.4 us  [fused(): pl.pallas_call(kernel, out_shape=jax.ShapeDtypeStruct((OWN, 2, LANES), f3...]
    reshape x3 -> x0, local copies, waits for them, and re-layouts: 2.89 us -> none  [the longest x2 1.45 us: body(): column_picks.reshape(RING_Y, RING_Z, OWN).transpose(1, 0, 2)]
    unnamed x0 -> x1, local copies, waits for them, and re-layouts: none -> 1.42 us
where the time goes in v3:
time: 42 us; the launch traced here: 41.9 us
  Pallas kernels  40.4 us (96%)
  local copies, waits for them, and re-layouts  1.42 us (3%)
    pallas_call x1, Pallas kernels, fused(): pl.pallas_call(kernel, out_shape=jax.ShapeDtypeStruct((OWN, 2, LANES), f3...  40.4 us
    unnamed x1, local copies, waits for them, and re-layouts  1.42 us

profile of v3, /device:TPU:1, one launch (start us, length us, event | category | flops | bytes accessed | tf_op | source)
XLA Modules:
  0.0 41.9 jit_solution(16022133074602770669)
XLA Ops:
  0.0 40.4 %shard_map.37 = f32[48,2,128]{2,1,0:T(2,128)} custom-call(f32[2,6144,128]{2,1,0:T(8,128)} %x_hbm.1, s32[6144]{0:T(1024)} %sign_ref.1, s32[1536]{0:T(1024)} %pick_ref.1), custom_call_target="tpu_custom_call" | custom-call | tf_op jit(solution)/shard_map/pallas_call | solution.py:343
  40.4 1.4 %copy.5 = f32[48,2,128]{2,1,0:T(2,128)} copy(f32[48,2,128]{2,1,0:T(2,128)} %shard_map.37) | data formatting | bytes 98304

commit v4 on v3

--- a/solution.py
+++ b/solution.py
@@ -20,22 +20,22 @@
 RING_Y = 4
 PANELS = 8
 OWN = SKETCH // (RING_Z * RING_Y)
-PART = OWN // 2
-BLOCK_A = PART * RING_Y
-BLOCK_B = PART * RING_Z
-START_B = BLOCK_A * RING_Z
+CLASSES = (("a", 24), ("b", 16), ("b", 8))
 TILE = 32
 FINE = jnp.float8_e4m3fn
 STEP = 512.0
-GROUPS = (
-    (("a", 3), ("a", -3), ("b", 2)),
-    (("a", 4), ("b", 1)),
-    (("a", 1), ("a", -1), ("b", -1)),
-    (("a", 2), ("a", -2)),
-    (("b", 0), ("a", 0)),
+PLAN = (
+    (((0, 4),), ((0, 4),)),
+    (((1, 2), (0, 3), (0, -3),), ((0, 3), (0, -3), (1, 2),)),
+    (((0, 1), (0, -1), (1, 1),), ((0, 1), (0, -1), (1, 1),)),
+    (((1, -1),), ((1, -1),)),
+    (((0, 2), (0, -2),), ((0, 2), (0, -2),)),
+    (((2, 2),), ((2, 2),)),
+    (((2, -1), (2, 1),), ((2, 1), (2, -1),)),
+    (((1, 0), (0, 0),), ((1, "own"),)),
+    (((2, 0),), ((2, "own"), (0, "own"),)),
 )
-
-
+BEARER = {4: 2, 3: 2, 2: 0, 1: 0}
 MESH = pl.DeviceIdType.MESH
 
 
@@ -53,27 +53,41 @@
     return 1.0 - 2.0 * sin * sin, 2.0 * sin * cos
 
 
+def block_rows(c):
+    kind, count = CLASSES[c]
+    return count * (RING_Y if kind == "a" else RING_Z)
+
+
+def first_of_owner(c):
+    return sum(count for _, count in CLASSES[:c])
+
+
+def class_row(c):
+    return first_of_owner(c) * RING_Y * RING_Z
+
+
 def table_row(column):
     owner, rest = divmod(column, OWN)
     y, z = divmod(owner, RING_Z)
-    if rest < PART:
-        return z * BLOCK_A + y * PART + rest
-    return START_B + y * BLOCK_B + z * PART + rest - PART
-
-
-def size(half):
-    return BLOCK_A if half == "a" else BLOCK_B
+    c = max(c for c in range(len(CLASSES)) if first_of_owner(c) <= rest)
+    kind, count = CLASSES[c]
+    rest = rest - first_of_owner(c)
+    if kind == "a":
+        return class_row(c) + (z * RING_Y + y) * count + rest
+    return class_row(c) + (y * RING_Z + z) * count + rest
 
 
 def rows_before(group):
-    return sum(size(half) for blocks in GROUPS[:group] for half, _ in blocks)
+    return sum(block_rows(c) for blocks, _ in PLAN[:group] for c, _ in blocks)
+
+
+MOST = max(rows_before(g + 1) - rows_before(g) for g in range(len(PLAN)))
 
 
 def kernel(
     x_hbm, sign_ref, pick_ref, out_ref,
-    x, fold, rhs_h, rhs_l, lhs_h, lhs_l, kb, w, pre, pad, tr, acc, sum_a, sum_b,
-    a_out, a_in, ya_in, b_out, b_in, zb_in, energy, n_in,
-    x_sem, a_send, a_recv, ya_send, ya_recv, b_send, b_recv, zb_send, zb_recv, n_send, n_recv,
+    x, fold, rhs_h, rhs_l, lhs_h, lhs_l, kb, w, pre, pad, tr, acc, energy, n_in,
+    x_sem, n_send, n_recv, out, into, second, total, sems,
 ):
     position = lax.axis_index("emit")
     panel = lax.axis_index("panel")
@@ -129,10 +143,12 @@
 
     odd = (2 * lax.broadcasted_iota(jnp.int32, (TILE, LANES), 1) + 1).astype(jnp.float32)
 
-    def source(half, d):
-        if half == "a":
-            return pl.multiple_of((z_here + d) % RING_Z * BLOCK_A, TILE)
-        return pl.multiple_of(START_B + (y_here + d) % RING_Y * BLOCK_B, TILE)
+    def source(c, d):
+        if CLASSES[c][0] == "a":
+            place = (z_here + d) % RING_Z
+        else:
+            place = (y_here + d) % RING_Y
+        return pl.multiple_of(class_row(c) + place * block_rows(c), TILE)
 
     def table_tile(first, row):
         sl = pl.ds(first, TILE)
@@ -151,16 +167,16 @@
                 lhs_l[to, DEPTH + lane : DEPTH + lane + LANES] = rest.astype(FINE)
 
     row = 0
-    for half, d in GROUPS[0]:
-        first = source(half, d)
-
-        @pl.loop(0, size(half) // TILE)
+    for c, d in PLAN[0][0]:
+        first = source(c, d)
+
+        @pl.loop(0, block_rows(c) // TILE)
         def _(t, first=first, row=row):
             table_tile(
                 pl.multiple_of(first + t * TILE, TILE), pl.multiple_of(row + t * TILE, TILE)
             )
 
-        row += size(half)
+        row += block_rows(c)
 
     peak = jnp.zeros((LANES, LANES), jnp.float32)
     for upper in range(SIGN_ROWS // 2, SIGN_ROWS):
@@ -200,17 +216,17 @@
     convert(INNER - 1)
 
     def work(group, refs):
-        blocks = GROUPS[group]
+        blocks = PLAN[group][0]
         start = rows_before(group)
-        count = sum(size(half) for half, _ in blocks)
+        count = rows_before(group + 1) - start
         tiles = []
-        if group + 1 < len(GROUPS):
+        if group + 1 < len(PLAN):
             row = start + count
-            for half, d in GROUPS[group + 1]:
-                first = source(half, d)
-                for t in range(0, size(half), TILE):
+            for c, d in PLAN[group + 1][0]:
+                first = source(c, d)
+                for t in range(0, block_rows(c), TILE):
                     tiles.append((pl.multiple_of(first + t, TILE), row + t))
-                row += size(half)
+                row += block_rows(c)
         for step in range(INNER):
             i = INNER - 1 - step
             product = jnp.dot(
@@ -223,10 +239,10 @@
             for first, row in tiles[len(tiles) * step // INNER : len(tiles) * (step + 1) // INNER]:
                 table_tile(first, row)
             first = 0
-            for (half, d), ref in zip(blocks, refs):
-                mine = slice(first, first + size(half))
-                first += size(half)
-                sl = pl.ds(source(half, d), size(half))
+            for (c, d), ref in zip(blocks, refs):
+                mine = slice(first, first + block_rows(c))
+                first += block_rows(c)
+                sl = pl.ds(source(c, d), block_rows(c))
                 new_real, new_imag = product[mine, :LANES], product[mine, LANES:]
                 if step:
                     real, imag = acc[mine, :LANES], acc[mine, LANES:]
@@ -252,70 +268,84 @@
         sent.append(copy)
         return copy
 
-    first_half = pl.ds(0, BLOCK_A // 2)
-    second_half = pl.ds(BLOCK_A // 2, BLOCK_A // 2)
     whole = slice(None)
-
-    def send_a(slot, out, to, part=whole):
-        return send(
-            a_out.at[out, part], a_in.at[slot, part], (a_send.at[slot], a_recv.at[slot]), at_z(to)
-        )
-
-    def send_b(d):
-        slot = d % RING_Y - 1
-        return send(b_out.at[slot], b_in.at[slot], (b_send.at[slot], b_recv.at[slot]), at_y(d))
-
-    work(0, [a_out.at[0], a_out.at[1], b_out.at[1]])
-    pl.semaphore_wait(barrier, len(partners))
-    near = [send_a(0, 0, 1), send_a(1, 1, -1)]
-    last_b = [send_b(2)]
-    work(1, [a_out.at[2], b_out.at[0]])
-    far = [send_a(2, 2, 2, first_half), send_a(3, 2, -2, second_half)]
-    last_b.append(send_b(1))
-    work(2, [a_out.at[3], a_out.at[4], b_out.at[2]])
-    last_a = [send_a(4, 3, 1), send_a(5, 4, -1)]
-    last_b.append(send_b(-1))
-    work(3, [a_out.at[5], a_out.at[6]])
-    for way, part in enumerate((first_half, second_half)):
-        near[way].wait_recv()
-        a_out[5 + way] += a_in[way]
-        far[way].wait_recv()
-        a_out[5 + way, part] += a_in[2 + way, part]
-        last_a.append(send_a(6 + way, 5 + way, 2 - 4 * way))
-    work(4, [sum_b, sum_a])
-
-    def own(ref, place):
-        return ref.at[pl.ds(pl.multiple_of(place * PART, PART), PART)]
-
-    for copy in last_b:
-        copy.wait_recv()
-    sum_b[...] += b_in[0] + b_in[1] + b_in[2]
-    copies_b = [
-        send(
-            own(sum_b, (z_here + d) % RING_Z), zb_in.at[d - 1],
-            (zb_send.at[d - 1], zb_recv.at[d - 1]), at_z(d),
-        )
-        for d in range(1, RING_Z)
-    ]
-    for copy in last_a:
-        copy.wait_recv()
-    sum_a[...] += (a_in[4] + a_in[5]) + (a_in[6] + a_in[7])
-    copies_a = [
-        send(
-            own(sum_a, (y_here + d) % RING_Y), ya_in.at[d - 1],
-            (ya_send.at[d - 1], ya_recv.at[d - 1]), at_y(d),
-        )
-        for d in range(1, RING_Y)
-    ]
-    raw_b = own(sum_b, z_here)[...]
-    for d, copy in enumerate(copies_b):
-        copy.wait_recv()
-        raw_b = raw_b + zb_in[d]
-    raw_a = own(sum_a, y_here)[...]
-    for d, copy in enumerate(copies_a):
-        copy.wait_recv()
-        raw_a = raw_a + ya_in[d]
-    raw = jnp.concatenate([raw_a, raw_b], axis=0)
+    sent_by = {}
+    last = {}
+
+    def out_ref_of(c, d):
+        if d == 0:
+            return total[c]
+        if CLASSES[c][0] == "b":
+            return out[c].at[d % RING_Y - 1]
+        return out[c].at[7 if d == 4 else abs(d) - 1 + (0 if d > 0 else 3)]
+
+    def half_of(c, way):
+        half = block_rows(c) // 2
+        return pl.ds(half * way, half)
+
+    def collect(c, way, far, ref):
+        for d in (4, 3, 2, 1):
+            if BEARER[d] == far:
+                part = half_of(c, way) if d == 4 else whole
+                sent_by[c, d, way].wait_recv()
+                ref[part] += into[c][2 * (d - 1) + way, part]
+
+    def leave(c, d):
+        kind, count = CLASSES[c]
+        if d == "own":
+            if kind == "a":
+                for way in range(2):
+                    collect(c, way, 0, total[c])
+                here, ring, device = y_here, RING_Y, at_y
+            else:
+                for slot in range(RING_Y - 1):
+                    sent_by[c, slot].wait_recv()
+                total[c][...] += into[c][0] + into[c][1] + into[c][2]
+                here, ring, device = z_here, RING_Z, at_z
+            last[c] = []
+            for away in range(1, ring):
+                start = pl.multiple_of((here + away) % ring * count, count)
+                last[c].append(
+                    send(
+                        total[c].at[pl.ds(start, count)], second[c].at[away - 1],
+                        (sems[c][2].at[away - 1], sems[c][3].at[away - 1]), device(away),
+                    )
+                )
+        elif kind == "b":
+            slot = d % RING_Y - 1
+            sent_by[c, slot] = send(
+                out[c].at[slot], into[c].at[slot], (sems[c][0].at[slot], sems[c][1].at[slot]), at_y(d)
+            )
+        else:
+            far = abs(d)
+            hops = far - BEARER[far]
+            for way in (0, 1) if d == 4 else (int(d < 0),):
+                part = half_of(c, way) if d == 4 else whole
+                ref = out_ref_of(c, d)
+                if far < 4:
+                    collect(c, way, far, ref)
+                slot = 2 * (far - 1) + way
+                sent_by[c, far, way] = send(
+                    ref.at[part], into[c].at[slot, part],
+                    (sems[c][0].at[slot], sems[c][1].at[slot]), at_z(hops - 2 * hops * way),
+                )
+
+    for g, (blocks, messages) in enumerate(PLAN):
+        work(g, [out_ref_of(c, d) for c, d in blocks])
+        if g == 0:
+            pl.semaphore_wait(barrier, len(partners))
+        for c, d in messages:
+            leave(c, d)
+
+    pieces = []
+    for c, (kind, count) in enumerate(CLASSES):
+        place = y_here if kind == "a" else z_here
+        piece = total[c][pl.ds(pl.multiple_of(place * count, count), count)]
+        for d, copy in enumerate(last[c]):
+            copy.wait_recv()
+            piece = piece + second[c][d]
+        pieces.append(piece)
+    raw = jnp.concatenate(pieces, axis=0)
 
     real, imag = raw[:, :LANES], raw[:, LANES:]
     pad[...] = jnp.zeros_like(pad)
@@ -361,28 +391,17 @@
             pltpu.VMEM((2, SKETCH, LANES), f32),
             pltpu.VMEM((LANES, LANES), f32),
             pltpu.VMEM((2, LANES, LANES), f32),
-            pltpu.VMEM((2 * BLOCK_A + BLOCK_B, wide), f32),
-            pltpu.VMEM((BLOCK_A, wide), f32),
-            pltpu.VMEM((BLOCK_B, wide), f32),
-            pltpu.VMEM((7, BLOCK_A, wide), f32),
-            pltpu.VMEM((8, BLOCK_A, wide), f32),
-            pltpu.VMEM((RING_Y - 1, PART, wide), f32),
-            pltpu.VMEM((RING_Y - 1, BLOCK_B, wide), f32),
-            pltpu.VMEM((RING_Y - 1, BLOCK_B, wide), f32),
-            pltpu.VMEM((RING_Z - 1, PART, wide), f32),
+            pltpu.VMEM((MOST, wide), f32),
             pltpu.VMEM((8, LANES), f32),
             pltpu.VMEM((PANELS - 1, 8, LANES), f32),
             pltpu.SemaphoreType.DMA((8,)),
-            pltpu.SemaphoreType.DMA((8,)),
-            pltpu.SemaphoreType.DMA((8,)),
-            pltpu.SemaphoreType.DMA((RING_Y - 1,)),
-            pltpu.SemaphoreType.DMA((RING_Y - 1,)),
-            pltpu.SemaphoreType.DMA((RING_Y - 1,)),
-            pltpu.SemaphoreType.DMA((RING_Y - 1,)),
-            pltpu.SemaphoreType.DMA((RING_Z - 1,)),
-            pltpu.SemaphoreType.DMA((RING_Z - 1,)),
             pltpu.SemaphoreType.DMA((PANELS - 1,)),
             pltpu.SemaphoreType.DMA((PANELS - 1,)),
+            [pltpu.VMEM((8 if kind == "a" else 3, block_rows(c), wide), f32) for c, (kind, _) in enumerate(CLASSES)],
+            [pltpu.VMEM((8 if kind == "a" else 3, block_rows(c), wide), f32) for c, (kind, _) in enumerate(CLASSES)],
+            [pltpu.VMEM((RING_Z - 1, count, wide), f32) for _, count in CLASSES],
+            [pltpu.VMEM((block_rows(c), wide), f32) for c in range(len(CLASSES))],
+            [[pltpu.SemaphoreType.DMA((8,))] * 4 for _ in CLASSES],
         ],
         compiler_params=pltpu.CompilerParams(
             collective_id=0, has_side_effects=True, vmem_limit_bytes=56 * 1024 * 1024

time: 42 us -> 40.7 us (0.969)
  Pallas kernels: 40.4 us -> 39 us
    pallas_call x1, Pallas kernels: 40.4 us -> 39 us  [fused(): pl.pallas_call(kernel, out_shape=jax.ShapeDtypeStruct((OWN, 2, LANES), f3...]
where the time goes in v4:
time: 40.7 us; the launch traced here: 40.5 us
  Pallas kernels  39 us (96%)
  local copies, waits for them, and re-layouts  1.42 us (3%)
    pallas_call x1, Pallas kernels, fused(): pl.pallas_call(kernel, out_shape=jax.ShapeDtypeStruct((OWN, 2, LANES), f3...  39 us
    unnamed x1, local copies, waits for them, and re-layouts  1.42 us

profile of v4, /device:TPU:1, one launch (start us, length us, event | category | flops | bytes accessed | tf_op | source)
XLA Modules:
  0.0 40.5 jit_solution(6092381348066999960)
XLA Ops:
  0.0 39.0 %shard_map.37 = f32[48,2,128]{2,1,0:T(2,128)} custom-call(f32[2,6144,128]{2,1,0:T(8,128)} %x_hbm.1, s32[6144]{0:T(1024)} %sign_ref.1, s32[1536]{0:T(1024)} %pick_ref.1), custom_call_target="tpu_custom_call" | custom-call | tf_op jit(solution)/shard_map/pallas_call | solution.py:373
  39.0 1.4 %copy.5 = f32[48,2,128]{2,1,0:T(2,128)} copy(f32[48,2,128]{2,1,0:T(2,128)} %shard_map.37) | data formatting | bytes 98304

commit v5 on v4

--- a/solution.py
+++ b/solution.py
@@ -25,13 +25,13 @@
 FINE = jnp.float8_e4m3fn
 STEP = 512.0
 PLAN = (
-    (((0, 4),), ((0, 4),)),
-    (((1, 2), (0, 3), (0, -3),), ((0, 3), (0, -3), (1, 2),)),
+    (((0, 4), (0, 3), (0, -3),), ((0, 4), (0, 3), (0, -3),)),
+    (((1, 2),), ((1, 2),)),
     (((0, 1), (0, -1), (1, 1),), ((0, 1), (0, -1), (1, 1),)),
     (((1, -1),), ((1, -1),)),
     (((0, 2), (0, -2),), ((0, 2), (0, -2),)),
     (((2, 2),), ((2, 2),)),
-    (((2, -1), (2, 1),), ((2, 1), (2, -1),)),
+    (((2, 1), (2, -1),), ((2, 1), (2, -1),)),
     (((1, 0), (0, 0),), ((1, "own"),)),
     (((2, 0),), ((2, "own"), (0, "own"),)),
 )

time: 40.7 us -> 40.5 us (level)
  no operation moved by 1% of the time
where the time goes in v5:
time: 40.5 us; the launch traced here: 40.3 us
  Pallas kernels  38.8 us (96%)
  local copies, waits for them, and re-layouts  1.42 us (4%)
    pallas_call x1, Pallas kernels, fused(): pl.pallas_call(kernel, out_shape=jax.ShapeDtypeStruct((OWN, 2, LANES), f3...  38.8 us
    unnamed x1, local copies, waits for them, and re-layouts  1.42 us

profile of v5, /device:TPU:1, one launch (start us, length us, event | category | flops | bytes accessed | tf_op | source)
XLA Modules:
  0.0 40.3 jit_solution(7690308393417481670)
XLA Ops:
  0.0 38.8 %shard_map.37 = f32[48,2,128]{2,1,0:T(2,128)} custom-call(f32[2,6144,128]{2,1,0:T(8,128)} %x_hbm.1, s32[6144]{0:T(1024)} %sign_ref.1, s32[1536]{0:T(1024)} %pick_ref.1), custom_call_target="tpu_custom_call" | custom-call | tf_op jit(solution)/shard_map/pallas_call | solution.py:373
  38.8 1.4 %copy.5 = f32[48,2,128]{2,1,0:T(2,128)} copy(f32[48,2,128]{2,1,0:T(2,128)} %shard_map.37) | data formatting | bytes 98304

commit v6 on v5

--- a/solution.py
+++ b/solution.py
@@ -131,6 +131,7 @@
     tr[0] = pad[...].T
     pad[0:SIGN_ROWS] = (2 * sign_ref[...].reshape(SIGN_ROWS, LANES) - 1).astype(jnp.float32)
     tr[1] = pad[...].T
+    pad[...] = jnp.zeros_like(pad)
     for q in range(PICK_ROWS):
         for slot, ref in enumerate(
             (kb.at[0], w.at[0], w.at[1], pre.at[0], pre.at[1], kb.at[1], kb.at[2])
@@ -348,7 +349,6 @@
     raw = jnp.concatenate(pieces, axis=0)
 
     real, imag = raw[:, :LANES], raw[:, LANES:]
-    pad[...] = jnp.zeros_like(pad)
     pad[:OWN] = real * real + imag * imag
     total = jnp.sum(pad[...].T, axis=0, keepdims=True)
     energy[...] = jnp.broadcast_to(total, energy.shape)

time: 40.5 us -> 40.4 us (level)
  no operation moved by 1% of the time
where the time goes in v6:
time: 40.4 us; the launch traced here: 40.3 us
  Pallas kernels  38.8 us (96%)
  local copies, waits for them, and re-layouts  1.42 us (4%)
    pallas_call x1, Pallas kernels, fused(): pl.pallas_call(kernel, out_shape=jax.ShapeDtypeStruct((OWN, 2, LANES), f3...  38.8 us
    unnamed x1, local copies, waits for them, and re-layouts  1.42 us

profile of v6, /device:TPU:1, one launch (start us, length us, event | category | flops | bytes accessed | tf_op | source)
XLA Modules:
  0.0 40.3 jit_solution(17875948375862744941)
XLA Ops:
  0.0 38.8 %shard_map.37 = f32[48,2,128]{2,1,0:T(2,128)} custom-call(f32[2,6144,128]{2,1,0:T(8,128)} %x_hbm.1, s32[6144]{0:T(1024)} %sign_ref.1, s32[1536]{0:T(1024)} %pick_ref.1), custom_call_target="tpu_custom_call" | custom-call | tf_op jit(solution)/shard_map/pallas_call | solution.py:373
  38.8 1.4 %copy.5 = f32[48,2,128]{2,1,0:T(2,128)} copy(f32[48,2,128]{2,1,0:T(2,128)} %shard_map.37) | data formatting | bytes 98304
